TPU v7x, 256 devices: a whole 4x4x8 slice. The times are simulated.
256 devices in a mesh: span: 4 (over x), dom: 64 (over z, y, core).
Axes of the slice: x: 4, y: 4, z: 8, core: 2. Of those that a mesh axis runs over, the one named last changes fastest.
Arguments:
- velocity: bfloat16 [3, 256, 81, 8192], P(None, 'span', None, 'dom'), may hold values from -6 to 6
- gradient: bfloat16 [3, 256, 81, 8192], P(None, 'span', None, 'dom'), may hold values from -6 to 6
- project_table: float32 [81, 32], replicated, may hold values from -0.89 to 0.89
- jacobian: float32 [8192], P('dom'), may hold values from 0.3 to 3
- stiff_elem: float32 [32, 32, 8192], P(None, None, 'dom'), may hold values from -0.05 to 3.2, as said below
- mass_elem: float32 [32, 32, 8192], P(None, None, 'dom'), may hold values from -0.025 to 1.6, as said below
- bound_map: int32 [32, 8192], P(None, 'dom'), may hold values from 0 to 2047
Outputs:
- solution_private: float32 [256, 114688], P('span', 'dom')
- solution_interface: float32 [256, 256], P('span')
Inputs may be any that keep to these rules, and one draw needn't show every extreme that they name: `bound_map`: entries below 1792 number unknowns private to the element's block of 128 elements; entries from 1792 on number the 256 interface unknowns that all blocks share. `stiff_elem`: symmetric with a dominant positive diagonal. `mass_elem`: symmetric with a dominant positive diagonal.
All inputs are finite; a program needn't handle non-finite values.
Results may differ from a plain program's by a relative error of at most 0.0003.
Values sent between devices are 32-bit elements; how exact they have to be, the bound alone decides.
A program may use at most 128 MiB of HBM per device.

v0:
```python
import jax
import jax.numpy as jnp
from jax import lax
from jax.sharding import PartitionSpec as P

ITERS = 3
NB = 1792
NIF = 256


time_step = 0.5
shift_base = 0.5
shift_slope = 8.0


def wave_index(index, size):
    return jnp.where(index == 1, size // 2, index // 2)


def dft_table(size):
    index = jnp.arange(size, dtype=jnp.int32)
    kappa = wave_index(index, size)
    phase = kappa[:, None] * index[None, :] % size
    angle = 2.0 * jnp.pi / size * phase.astype(jnp.float32)
    scale = jnp.where(index < 2, jnp.sqrt(1.0 / size), jnp.sqrt(2.0 / size)).astype(jnp.float32)
    odd_rows = (index % 2 == 1) & (index != 1)
    values = jnp.where(odd_rows[:, None], -jnp.sin(angle), jnp.cos(angle))
    return values * scale[:, None]


def make_forcing(velocity, gradient):
    advect = velocity[0].astype(jnp.float32) * gradient[0].astype(jnp.float32)
    advect = advect + velocity[1].astype(jnp.float32) * gradient[1].astype(jnp.float32)
    advect = advect + velocity[2].astype(jnp.float32) * gradient[2].astype(jnp.float32)
    return velocity[0].astype(jnp.float32) - time_step * advect


def inner(left, right):
    return (jnp.sum(left[0] * right[0], axis=1), jnp.sum(left[1] * right[1], axis=1))


def axpy(first, factor, second):
    return (first[0] + factor[:, None] * second[0], first[1] + factor[:, None] * second[1])


def shards(velocity, gradient, project_table, jacobian, stiff_elem, mass_elem, bound_map):
    high = lax.Precision.HIGHEST
    planes = velocity.shape[1]
    size = planes * lax.axis_size("span")
    forcing = make_forcing(velocity, gradient)
    table = dft_table(size)
    spectra = jnp.einsum(
        "mz,zqe->mqe",
        table,
        lax.all_to_all(forcing, "span", split_axis=2, concat_axis=0, tiled=True),
        precision=high,
    )
    spectra = lax.all_to_all(spectra, "span", split_axis=0, concat_axis=2, tiled=True)
    load = jnp.einsum("qb,mqe->mbe", project_table, spectra, precision=high) * jacobian
    first_mode = lax.axis_index("span") * planes
    modes = first_mode + jnp.arange(planes, dtype=jnp.int32)
    kappa = wave_index(modes, size).astype(jnp.float32)
    shift = shift_base + shift_slope * (kappa / size) ** 2
    flat = bound_map.reshape(-1)

    def assemble(values):
        local = (
            jnp.zeros((planes, NB + NIF), jnp.float32).at[:, flat].add(values.reshape(planes, -1))
        )
        shared = lax.psum(local[:, NB:], "dom")
        return (local[:, :NB], shared)

    rhs = assemble(load)
    solution = (jnp.zeros_like(rhs[0]), jnp.zeros_like(rhs[1]))
    residual = rhs

    def squares_of(vector):
        own, shared = inner(vector, vector)
        return lax.psum(own, "dom") + shared

    direction = rhs
    norm_now = squares_of(residual)
    for step in range(ITERS):
        whole = jnp.concatenate([direction[0], direction[1]], axis=1)
        gathered = whole[:, bound_map]
        first = jnp.einsum("cbe,mbe->mce", stiff_elem, gathered, precision=high)
        second = jnp.einsum("cbe,mbe->mce", mass_elem, gathered, precision=high)
        image = assemble(first + shift[:, None, None] * second)
        own, shared = inner(direction, image)
        alpha = norm_now / (lax.psum(own, "dom") + shared)
        solution = axpy(solution, alpha, direction)
        residual = axpy(residual, -alpha, image)
        norm_next = squares_of(residual)
        direction = axpy(residual, norm_next / norm_now, direction)
        norm_now = norm_next
    return (solution[0], solution[1])


def solution(mesh):
    return jax.shard_map(
        shards,
        mesh=mesh,
        in_specs=(
            P(None, "span", None, "dom"),
            P(None, "span", None, "dom"),
            P(),
            P("dom"),
            P(None, None, "dom"),
            P(None, None, "dom"),
            P(None, "dom"),
        ),
        out_specs=(P("span", "dom"), P("span", None)),
        check_vma=False,
    )
```

profile of v0, /device:TPU:1, one launch (start us, length us, event | category | flops | bytes accessed | tf_op | source)
XLA Modules:
  0.0 1339.7 jit_solution(7651132376806668913)
XLA Ops:
  7.2 4.6 fusion.74
  11.7 3.4 copy.85
  15.1 4.3 fusion.75
  19.5 4.1 copy.86
  23.6 4.1 copy.87
  27.7 4.1 copy.88
  31.8 3.0 copy.89
  34.9 4.1 copy.90
  39.0 9.0 convert_subtract_fusion
  48.0 5.3 all-to-all-start
  53.3 46.9 %all-to-all-done = f32[64,81,128]{1,0,2:T(8,128)} async-done(((f32[64,81,128]{1,0,2:T(8,128)}), f32[64,81,128]{1,0,2:T(8,128)}, u32[]{:S(2)}, u32[]{:S(2)}) %all-to-all-start) | async-done | bytes 2654240 | tf_op jit(solution)/shard_map/all_to_all | solution.py:55
  100.2 4.6 copy.59
  104.9 9.3 fusion.3
  114.1 3.8 copy.61
  117.9 5.0 all-to-all-start.1
  123.0 45.3 %all-to-all-done.1 = f32[256,81,32]{1,2,0:T(8,128)} async-done(((f32[256,81,32]{1,2,0:T(8,128)}), f32[256,81,32]{1,2,0:T(8,128)}, u32[]{:S(2)}, u32[]{:S(2)}) %all-to-all-start.1) | async-done | bytes 2654240 | tf_op jit(solution)/shard_map/all_to_all | solution.py:58
  168.3 2.8 copy.62
  171.1 4.4 fusion.29
  175.6 2.1 copy.84
  177.7 22.9 %scatter_custom_fusion = f32[64,2048]{0,1:T(8,128)S(1)} fusion(s32[4096]{0:T(1024)S(1)} %bitcast.109, f32[4096,64]{1,0:T(8,128)} %bitcast.107, f32[]{:T(128)} %constant.69.clone.1), kind=kCustom, calls=%fused_computation.61 | custom fusion | flops 262144 | bytes 524800 | tf_op jit(solution)/shard_map/scatter-add | solution.py:68
  201.4 2.9 copy.66
  204.3 3.9 copy.67
  209.1 172.6 %all-reduce.6.cloned.1.call-done = f32[64,256]{0,1:T(8,128)} async-done(((f32[64,256]{0,1:T(8,128)}), f32[64,256]{0,1:T(8,128)}) %all-reduce.6.cloned.1.call-update) | async-done | bytes 65552 | tf_op jit(solution)/shard_map/psum | solution.py:70
  381.8 1.3 pad_maximum_fusion
  383.1 14.3 %gather_fusion = f32[4096,64]{1,0:T(8,128)} fusion(f32[64,2048]{0,1:T(8,128)S(1)} %pad_maximum_fusion, s32[4096]{0:T(1024)S(1)} %fusion.62), kind=kCustom, calls=%fused_computation | custom fusion | bytes 2113536 | tf_op jit(solution)/shard_map/gather | solution.py:85
  397.4 5.0 fusion.13
  402.5 4.7 add_bitcast_fusion.2
  407.2 3.0 copy.68
  410.2 1.6 copy.131
  411.8 3.2 copy.69
  415.1 23.7 %scatter_custom_fusion.1 = f32[64,2048]{0,1:T(8,128)} fusion(s32[4096]{0:T(1024)S(1)} %bitcast.110, f32[4096,64]{1,0:T(8,128)} %copy.69, f32[]{:T(128)} %constant.69.clone.1), kind=kCustom, calls=%fused_computation.59 | custom fusion | flops 262144 | bytes 524800 | tf_op jit(solution)/shard_map/scatter-add | solution.py:68
  438.8 1.6 slice.66
  440.4 1.4 multiply_reduce_fusion.3
  441.8 122.6 %all-reduce = (f32[64]{0:T(128)S(1)}, f32[64]{0:T(128)S(1)}) all-reduce(f32[64]{0:T(128)S(1)} %get-tuple-element.9, f32[64]{0:T(128)S(1)} %get-tuple-element.8), channel_id=1, replica_groups=mesh['span'=4,'dom'=64] {'dom'}, use_global_device_ids=true, to_apply=%region_2.3 | all-reduce | flops 128 | bytes 1024 | tf_op jit(solution)/shard_map/psum | solution.py:79
  564.5 46.6 %all-reduce.8.cloned.1.call-done = f32[64,256]{0,1:T(8,128)} async-done(((f32[64,256]{0,1:T(8,128)}), f32[64,256]{0,1:T(8,128)}) %all-reduce.8.cloned.1.call-update) | async-done | bytes 65552 | tf_op jit(solution)/shard_map/psum | solution.py:70
  612.7 2.3 multiply_reduce_fusion.2
  615.0 123.0 %psum.74 = f32[64]{0:T(128)S(1)} all-reduce(f32[64]{0:T(128)S(1)} %get-tuple-element.22), channel_id=1, replica_groups=mesh['span'=4,'dom'=64] {'dom'}, use_global_device_ids=true, to_apply=%region_11.12 | all-reduce | flops 64 | bytes 512 | tf_op jit(solution)/shard_map/psum | solution.py:79
  738.7 1.3 multiply_add_fusion.3
  741.0 14.1 %gather_fusion.1 = f32[4096,64]{1,0:T(8,128)} fusion(f32[64,2048]{0,1:T(8,128)S(1)} %pad_maximum_fusion.1, s32[4096]{0:T(1024)S(1)} %copy-done.23), kind=kCustom, calls=%fused_computation.1 | custom fusion | bytes 2113536 | tf_op jit(solution)/shard_map/gather | solution.py:85
  755.1 5.0 fusion.9
  760.1 4.7 add_bitcast_fusion.1
  764.8 3.0 copy.73
  767.8 1.6 copy.130
  769.5 3.2 copy.74
  772.7 23.7 %scatter_custom_fusion.2 = f32[64,2048]{0,1:T(8,128)} fusion(s32[4096]{0:T(1024)} %bitcast.111, f32[4096,64]{1,0:T(8,128)} %copy.74, f32[]{:T(128)} %constant.69.clone.1), kind=kCustom, calls=%fused_computation.57 | custom fusion | flops 262144 | bytes 524800 | tf_op jit(solution)/shard_map/scatter-add | solution.py:68
  796.4 1.6 slice.68
  798.0 1.4 multiply_reduce_fusion.1
  799.4 126.9 %psum.75 = f32[64]{0:T(128)} all-reduce(f32[64]{0:T(128)S(1)} %multiply_reduce_fusion.1), channel_id=1, replica_groups=mesh['span'=4,'dom'=64] {'dom'}, use_global_device_ids=true, to_apply=%region_15.16 | all-reduce | flops 64 | bytes 512 | tf_op jit(solution)/shard_map/psum | solution.py:90
  926.4 44.0 %all-reduce.10.cloned.1.call-done = f32[64,256]{0,1:T(8,128)} async-done(((f32[64,256]{0,1:T(8,128)}), f32[64,256]{0,1:T(8,128)}) %all-reduce.10.cloned.1.call-update) | async-done | bytes 65552 | tf_op jit(solution)/shard_map/psum | solution.py:70
  973.1 2.2 multiply_reduce_fusion
  975.3 123.2 %psum.77 = f32[64]{0:T(128)} all-reduce(f32[64]{0:T(128)} %multiply_reduce_fusion), channel_id=1, replica_groups=mesh['span'=4,'dom'=64] {'dom'}, use_global_device_ids=true, to_apply=%region_19.20 | all-reduce | flops 64 | bytes 512 | tf_op jit(solution)/shard_map/psum | solution.py:79
  1099.3 1.3 fusion.70
  1100.6 1.6 multiply_add_fusion.1
  1103.2 14.1 %gather_fusion.2 = f32[4096,64]{1,0:T(8,128)} fusion(f32[64,2048]{0,1:T(8,128)S(1)} %pad_maximum_fusion.2, s32[4096]{0:T(1024)S(1)} %copy-done.23), kind=kCustom, calls=%fused_computation.2 | custom fusion | bytes 2113536 | tf_op jit(solution)/shard_map/gather | solution.py:85
  1117.3 5.0 fusion.5
  1122.4 3.5 add_bitcast_fusion
  1125.8 1.6 copy.78
  1128.1 2.0 copy.79
  1130.1 23.8 %scatter_custom_fusion.3 = f32[64,2048]{0,1:T(8,128)} fusion(s32[4096]{0:T(1024)} %bitcast.112, f32[4096,64]{1,0:T(8,128)} %copy.79, f32[]{:T(128)} %constant.69.clone.1), kind=kCustom, calls=%fused_computation.55 | custom fusion | flops 262144 | bytes 524800 | tf_op jit(solution)/shard_map/scatter-add | solution.py:68
  1153.8 1.6 slice.70
  1155.4 1.4 fusion.30
  1156.9 126.3 %psum.78 = f32[64]{0:T(128)S(1)} all-reduce(f32[64]{0:T(128)S(1)} %fusion.30), channel_id=1, replica_groups=mesh['span'=4,'dom'=64] {'dom'}, use_global_device_ids=true, to_apply=%region_23.24 | all-reduce | flops 64 | bytes 512 | tf_op jit(solution)/shard_map/psum | solution.py:90
  1283.1 44.8 %all-reduce.12.cloned.1.call-done = f32[64,256]{0,1:T(8,128)} async-done(((f32[64,256]{0,1:T(8,128)}), f32[64,256]{0,1:T(8,128)}) %all-reduce.12.cloned.1.call-update) | async-done | bytes 65552 | tf_op jit(solution)/shard_map/psum | solution.py:70
  1330.8 2.2 copy.80
  (103 shorter events, 13.3 us)
Async XLA Ops:
  7.2 164.0 %copy-start = (f32[81,32]{0,1:T(8,128)S(1)}, f32[81,32]{0,1:T(8,128)}, u32[]{:S(2)}) copy-start(f32[81,32]{0,1:T(8,128)} %param.9) | copy-start | bytes 31108
  48.0 52.3 %all-to-all-start = ((f32[64,81,128]{1,0,2:T(8,128)}), f32[64,81,128]{1,0,2:T(8,128)}, u32[]{:S(2)}, u32[]{:S(2)}) async-start(f32[64,81,128]{1,0,2:T(8,128)} %convert_subtract_fusion), calls=%async_computation | async-start | bytes 8388608 | tf_op jit(solution)/shard_map/all_to_all | solution.py:55
  117.9 5.1 copy-start.24
  117.9 50.4 %all-to-all-start.1 = ((f32[256,81,32]{1,2,0:T(8,128)}), f32[256,81,32]{1,2,0:T(8,128)}, u32[]{:S(2)}, u32[]{:S(2)}) async-start(f32[256,81,32]{1,2,0:T(8,128)} %copy.61), calls=%async_computation.1 | async-start | bytes 8388608 | tf_op jit(solution)/shard_map/all_to_all | solution.py:58
  122.9 258.9 %all-reduce.6.cloned.1.call-start = ((), (), s32[]{:S(2)}) async-start(), calls=%async_computation.2 | async-start | bytes 262144 | tf_op jit(solution)/shard_map/psum | solution.py:70
  123.0 260.1 %copy-start.22 = (s32[4096]{0:T(1024)}, s32[4096]{0:T(1024)S(1)}, u32[]{:S(2)}) copy-start(s32[4096]{0:T(1024)S(1)} %fusion.62) | copy-start | bytes 49156
  123.0 292.1 %copy-start.25 = (s32[4096,1]{0,1:T(1,128)}, s32[4096,1]{0,1:T(1,128)S(1)}, u32[]{:S(2)}) copy-start(s32[4096,1]{0,1:T(1,128)S(1)} %compare_select_fusion) | copy-start | bytes 49156
  168.3 2.9 copy-start.34
  200.6 7.6 copy-start.5
  201.3 409.8 %all-reduce.8.cloned.1.call-start = ((), (), s32[]{:S(2)}) async-start(), calls=%async_computation.3 | async-start | bytes 262144 | tf_op jit(solution)/shard_map/psum | solution.py:70
  201.4 201.1 %copy-start.28 = (f32[64]{0:T(128)}, f32[64]{0:T(128)S(1)}, u32[]{:S(2)}) copy-start(f32[64]{0:T(128)S(1)} %multiply_add_fusion.10) | copy-start | bytes 772
  397.4 5.0 copy-start.2
  397.4 5.0 copy-start.14
  411.8 28.6 %copy-start.6 = (f32[64,2048]{0,1:T(8,128)S(1)}, f32[64,2048]{0,1:T(8,128)}, u32[]{:S(2)}) copy-start(f32[64,2048]{0,1:T(8,128)} %copy-done.5) | copy-start | bytes 1572868
  415.1 196.0 %copy-start.16 = (f32[64,256]{0,1:T(8,128)S(1)}, f32[64,256]{0,1:T(8,128)}, u32[]{:S(2)}) copy-start(f32[64,256]{0,1:T(8,128)} %all-reduce.6.cloned.1.call-done) | copy-start | bytes 196612
  440.3 530.0 %all-reduce.10.cloned.1.call-start = ((), (), s32[]{:S(2)}) async-start(), calls=%async_computation.4 | async-start | bytes 262144 | tf_op jit(solution)/shard_map/psum | solution.py:70
  611.1 126.9 %copy-start.21 = (f32[64,256]{0,1:T(8,128)S(1)}, f32[64,256]{0,1:T(8,128)}, u32[]{:S(2)}) copy-start(f32[64,256]{0,1:T(8,128)} %all-reduce.8.cloned.1.call-done) | copy-start | bytes 196612
  738.1 360.5 %copy-start.17 = (f32[64,256]{0,1:T(8,128)}, f32[64,256]{0,1:T(8,128)S(1)}, u32[]{:S(2)}) copy-start(f32[64,256]{0,1:T(8,128)S(1)} %get-tuple-element.21) | copy-start | bytes 196612
  738.7 2.3 copy-start.23
  739.9 0.9 copy-start.8
  755.1 5.0 copy-start.3
  755.1 5.0 copy-start.15
  755.1 5.0 copy-start.29
  769.5 28.5 %copy-start.9 = (f32[64,1792]{0,1:T(8,128)S(1)}, f32[64,1792]{0,1:T(8,128)}, u32[]{:S(2)}) copy-start(f32[64,1792]{0,1:T(8,128)} %copy-done.8) | copy-start | bytes 1376260
  797.9 530.0 %all-reduce.12.cloned.1.call-start = ((), (), s32[]{:S(2)}) async-start(), calls=%async_computation.5 | async-start | bytes 262144 | tf_op jit(solution)/shard_map/psum | solution.py:70
  970.4 128.2 %copy-start.19 = (f32[64,256]{0,1:T(8,128)S(1)}, f32[64,256]{0,1:T(8,128)}, u32[]{:S(2)}) copy-start(f32[64,256]{0,1:T(8,128)} %all-reduce.10.cloned.1.call-done) | copy-start | bytes 196612
  972.5 0.6 copy-start.26
  1098.5 3.6 copy-start.20
  1098.6 3.7 copy-start.27
  1099.3 2.9 copy-start.18
  1102.2 0.9 copy-start.11
  1117.3 5.0 copy-start.4
  1117.3 5.0 copy-start.13
  1117.3 5.0 copy-start.30
  1128.1 27.4 %copy-start.12 = (f32[64,1792]{0,1:T(8,128)S(1)}, f32[64,1792]{0,1:T(8,128)}, u32[]{:S(2)}) copy-start(f32[64,1792]{0,1:T(8,128)} %copy-done.11) | copy-start | bytes 1376260
  1130.0 198.8 %copy-start.33 = (f32[64]{0:T(128)S(1)}, f32[64]{0:T(128)}, u32[]{:S(2)}) copy-start(f32[64]{0:T(128)} %get-tuple-element.15) | copy-start | bytes 772
  1130.0 198.8 %copy-start.7 = (f32[64,2048]{0,1:T(8,128)S(1)}, f32[64,2048]{0,1:T(8,128)}, u32[]{:S(2)}) copy-start(f32[64,2048]{0,1:T(8,128)} %copy-done.5) | copy-start | bytes 1572868
  1130.0 198.9 %copy-start.10 = (f32[64,1792]{0,1:T(8,128)S(1)}, f32[64,1792]{0,1:T(8,128)}, u32[]{:S(2)}) copy-start(f32[64,1792]{0,1:T(8,128)} %copy-done.8) | copy-start | bytes 1376260
  1130.0 198.9 %copy-start.31 = (f32[64]{0:T(128)S(1)}, f32[64]{0:T(128)}, u32[]{:S(2)}) copy-start(f32[64]{0:T(128)} %get-tuple-element.25) | copy-start | bytes 772
  1130.1 198.9 %copy-start.32 = (f32[64]{0:T(128)S(1)}, f32[64]{0:T(128)}, u32[]{:S(2)}) copy-start(f32[64]{0:T(128)} %get-tuple-element.17) | copy-start | bytes 772
  1328.9 4.1 copy-start.1
Sparse Core Ops, SparseCore 0:
  201.4 180.2 all-reduce.5
  440.5 170.5 all-reduce.7
  798.1 172.2 all-reduce.9
  1155.6 172.3 all-reduce.11
where the time goes:
time: 1350 us; the launch traced here: 1340 us
  blocking collectives  622 us (46%)
  waiting for transfers between devices  400 us (30%)
  local copies, waits for them, and re-layouts  126 us (9%)
  other arithmetic  125 us (9%)
  matrix products  41.6 us (3%)
  between operations  14.5 us (1%)
    psum x3, blocking collectives, squares_of(): return lax.psum(own, 'dom') + shared  369 us
    psum x4, waiting for transfers between devices, assemble(): shared = lax.psum(local[:, NB:], 'dom')  308 us
    psum x2, blocking collectives, shards(): alpha = norm_now / (lax.psum(own, 'dom') + shared)  253 us
    scatter-add x4, other arithmetic, assemble(): jnp.zeros((planes, NB + NIF), jnp.float32).at[:, flat]  94 us
    all_to_all x1, waiting for transfers between devices, shards(): lax.all_to_all(forcing, 'span', split_axis=2, concat_axis=0, tiled=True)  46.9 us
    all_to_all x1, waiting for transfers between devices, shards(): lax.all_to_all(spectra, 'span', split_axis=0, concat_axis=2, tiled=True)  45.3 us
    gather x3, local copies, waits for them, and re-layouts, shards(): gathered = whole[:, bound_map]  42.5 us
    unnamed x83, local copies, waits for them, and re-layouts  39 us
  transfers between devices with their start and end apart: 6, of which 6 were waited for; matrix products, arithmetic and copies ran while one was open for 1% of the time, Pallas kernels for 0%

commit v1 on v0

v1 whole, which is shorter than its diff:
```python
import jax
import jax.numpy as jnp
import numpy as np
from jax import lax
from jax.experimental import pallas as pl
from jax.experimental.pallas import tpu as pltpu
from jax.sharding import PartitionSpec as P

MESH = pl.DeviceIdType.MESH
F32 = jnp.float32
BF16 = jnp.bfloat16
QP = 81
NBE = 32
ED = 128
PLANES = 64
SIZE = 256
SPAN = 4
TILES = 8
TILE = 256
PRIV = 1792
GROUP = 8
WIDE = TILE + 128
QCHUNK = 9
NT = (((1,), (1,)), ((), ()))


def spanwise_table():
    index = np.arange(SIZE)
    kappa = np.where(index == 1, SIZE // 2, index // 2)
    angle = 2.0 * np.pi / SIZE * ((kappa[:, None] * index[None, :]) % SIZE)
    scale = np.where(index < 2, np.sqrt(1.0 / SIZE), np.sqrt(2.0 / SIZE))
    odd = (index % 2 == 1) & (index != 1)
    return (np.where(odd[:, None], -np.sin(angle), np.cos(angle)) * scale[:, None]).astype(np.float32)


def split(values):
    high = values.astype(BF16)
    return high, (values - high.astype(F32)).astype(BF16)


def both(product):
    half = product.shape[0] // 2
    return product[:half] + product[half:]


def dot(left, right):
    return jnp.dot(left, right, preferred_element_type=F32)


def kernel(
    vel_hbm, grad_hbm, project, jacobian, stiff, mass, bmap, table,
    out_private, out_interface,
    vel, grad, forcing, planes, hot, parts, vparts, gathered_w, gathered_a, gathered_r,
    w8, a8, p8, r8, x8, send8, cross, modes,
    msg, recv_a, recv_b, full,
    in_sem, span_send, span_recv, dom_send, dom_recv,
):
    s = lax.axis_index("span")
    d = lax.axis_index("dom")
    zi = lax.div(d, GROUP)
    i = lax.rem(d, GROUP)

    def chunk_copies(chunk):
        rows = pl.ds(chunk * QCHUNK, QCHUNK)
        return [
            pltpu.make_async_copy(src.at[:, rows], dst.at[:, rows], in_sem.at[which, chunk])
            for which, (src, dst) in enumerate(((vel_hbm, vel), (grad_hbm, grad)))
        ]

    for chunk in range(QP // QCHUNK):
        for copy in chunk_copies(chunk):
            copy.start()

    barrier = pltpu.get_barrier_semaphore()
    for k in range(1, GROUP):
        pl.semaphore_signal(barrier, inc=1, device_id=(s, zi * GROUP + lax.rem(i + k, GROUP)), device_id_type=MESH)
        pl.semaphore_signal(barrier, inc=1, device_id=(s, lax.rem(zi + k, GROUP) * GROUP + i), device_id_type=MESH)
    for k in range(1, SPAN):
        pl.semaphore_signal(barrier, inc=1, device_id=(lax.rem(s + k, SPAN), d), device_id_type=MESH)

    @pl.loop(0, NBE)
    def _(b):
        here = bmap[pl.ds(b, 1), :]
        for g in range(0, PRIV + TILE, 256):
            rows = lax.broadcasted_iota(jnp.int32, (256, ED), 0) + g
            hot[pl.ds(g, 256), pl.ds(pl.multiple_of(b * ED, ED), ED)] = jnp.where(rows == here, 1.0, 0.0).astype(BF16)

    @pl.loop(0, QP // QCHUNK)
    def _(chunk):
        for copy in chunk_copies(chunk):
            copy.wait()

        @pl.loop(0, QCHUNK)
        def _(step):
            q = chunk * QCHUNK + step
            first = vel[0, q].astype(F32)
            advect = first * grad[0, q].astype(F32)
            advect = advect + vel[1, q].astype(F32) * grad[1, q].astype(F32)
            advect = advect + vel[2, q].astype(F32) * grad[2, q].astype(F32)
            forcing[pl.ds(pl.multiple_of(q * PLANES, PLANES), PLANES), :] = first - 0.5 * advect

    project_high, project_low = split(project[...])
    project_both = jnp.concatenate([project_high, project_low], axis=0)
    area = jnp.concatenate([jacobian[...], jacobian[...]], axis=1)

    @pl.loop(0, PLANES // 2)
    def _(pair):
        values = jnp.concatenate(
            [forcing[pl.ds(2 * pair + k, QP, stride=PLANES), :] for k in range(2)], axis=1
        )
        high, low = split(values)
        load = (both(dot(project_both, high)) + dot(project_high, low)) * area
        start = pl.multiple_of(pair * 2 * NBE, 2 * NBE)
        planes[pl.ds(start, NBE), :] = load[:, :ED]
        planes[pl.ds(start + NBE, NBE), :] = load[:, ED:]

    @pl.loop(0, NBE)
    def _(b):
        high, low = split(planes[pl.ds(b, PLANES, stride=NBE), :])
        columns = pl.ds(pl.multiple_of(b * ED, ED), ED)
        parts[:PLANES, columns] = high
        parts[PLANES:, columns] = low

    def assemble(tile):
        rows = pl.ds(pl.multiple_of(tile * TILE, TILE), TILE)
        return both(lax.dot_general(parts[...], hot[rows, :], NT, preferred_element_type=F32))

    pl.semaphore_wait(barrier, 2 * (GROUP - 1) + SPAN - 1)
    out_copies = []
    for k in (2, 1, 3, 0):
        j = lax.rem(s + k, SPAN)

        @pl.loop(0, 2)
        def _(half, j=j):
            send8[2 * j + half] = assemble(2 * j + half)

        rows = pl.ds(pl.multiple_of(s * PLANES, PLANES), PLANES)
        if k:
            copy = pltpu.make_async_remote_copy(
                src_ref=send8.at[pl.ds(2 * j, 2)], dst_ref=cross.at[:, rows],
                send_sem=span_send.at[0, k], recv_sem=span_recv.at[0, k],
                device_id=(j, d), device_id_type=MESH,
            )
            copy.start()
            out_copies.append(copy)
        else:
            cross[:, rows, :] = send8[pl.ds(2 * j, 2)]
    for copy in out_copies:
        copy.wait_recv()

    for half in range(2):
        high, low = split(cross[half])
        modes[half] = both(dot(table[...], high)) + dot(table[:SIZE, :], low)
    back_copies = []
    for k in (2, 1, 3):
        j = lax.rem(s + k, SPAN)
        copy = pltpu.make_async_remote_copy(
            src_ref=modes.at[:, pl.ds(pl.multiple_of(j * PLANES, PLANES), PLANES)], dst_ref=r8.at[pl.ds(2 * s, 2)],
            send_sem=span_send.at[1, k], recv_sem=span_recv.at[1, k],
            device_id=(j, d), device_id_type=MESH,
        )
        copy.start()
        back_copies.append(copy)
    r8[pl.ds(2 * s, 2)] = modes[:, pl.ds(pl.multiple_of(s * PLANES, PLANES), PLANES), :]
    for copy in back_copies:
        copy.wait_recv()

    def dom_sum(inst, start, width, works):
        columns = pl.ds(start, width)

        def rows_of(index):
            return pl.ds(pl.multiple_of(index * 8, 8), 8)

        def run(stage, copies):
            for copy in copies:
                copy.start()
            works[stage]()
            for copy in copies:
                copy.wait_recv()
            return copies

        def remote(stage, k, src, dst, target):
            return pltpu.make_async_remote_copy(
                src_ref=src, dst_ref=dst, send_sem=dom_send.at[inst, stage, k], recv_sem=dom_recv.at[inst, stage, k],
                device_id=(s, target), device_id_type=MESH,
            )

        copies = []
        for k in range(1, GROUP):
            peer = lax.rem(i + k, GROUP)
            copies.append(remote(0, k, msg.at[inst, rows_of(peer), columns], recv_a.at[inst, k, :, columns], zi * GROUP + peer))
        done = run(0, copies)
        total = msg[inst, rows_of(i), columns]
        for k in range(1, GROUP):
            total = total + recv_a[inst, k, :, columns]
        recv_b[inst, zi, :, columns] = total
        copies = []
        for k in range(1, GROUP):
            peer = lax.rem(zi + k, GROUP)
            own = recv_b.at[inst, zi, :, columns]
            copies.append(remote(1, k, own, own, peer * GROUP + i))
        done = done + run(1, copies)
        total = recv_b[inst, 0, :, columns]
        for k in range(1, GROUP):
            total = total + recv_b[inst, k, :, columns]
        full[inst, rows_of(i), columns] = total
        copies = []
        for k in range(1, GROUP):
            own = full.at[inst, rows_of(i), columns]
            copies.append(remote(2, k, own, own, zi * GROUP + lax.rem(i + k, GROUP)))
        done = done + run(2, copies)
        for copy in done:
            copy.wait_send()

    def keep_parts(tile, values):
        high, low = split(values)
        columns = pl.ds(pl.multiple_of(tile * TILE, TILE), TILE)
        vparts[:PLANES, columns] = high
        vparts[PLANES:, columns] = low

    def gather_private(first, last):
        @pl.loop(first, last)
        def _(n):
            columns = pl.ds(pl.multiple_of(n * TILE, TILE), TILE)
            out = both(dot(vparts[:, :PRIV], hot[:PRIV, columns]))
            gathered_w[2 * n] = out[:, :ED]
            gathered_w[2 * n + 1] = out[:, ED:]

    def gather_interface(values):
        keep_parts(TILES - 1, values)
        lhs = vparts[:, PRIV:]

        @pl.loop(0, NBE // 2)
        def _(n):
            columns = pl.ds(pl.multiple_of(n * TILE, TILE), TILE)
            out = both(dot(lhs, hot[PRIV:, columns]))
            gathered_w[2 * n] += out[:, :ED]
            gathered_w[2 * n + 1] += out[:, ED:]

    def assemble_private(first, last):
        @pl.loop(first, last)
        def _(tile):
            values = assemble(tile)
            w8[tile] = values
            keep_parts(tile, values)

    def nothing():
        pass

    lane = lax.broadcasted_iota(jnp.int32, (PLANES, 128), 1)
    mode = lax.broadcasted_iota(jnp.int32, (PLANES, 128), 0) + s * PLANES
    kappa = jnp.where(mode == 1, SIZE // 2, lax.shift_right_logical(mode, 1)).astype(F32) * (1.0 / SIZE)
    shift = 0.5 + 8.0 * kappa * kappa

    def operate(source):
        def column(c, products):
            first = jnp.zeros((PLANES, ED), F32)
            second = jnp.zeros((PLANES, ED), F32)
            for b in range(NBE):
                values = source[b]
                first = first + stiff[c, pl.ds(b, 1), :] * values
                second = second + mass[c, pl.ds(b, 1), :] * values
            image = first + shift * second
            high, low = split(image)
            columns = pl.ds(pl.multiple_of(c * ED, ED), ED)
            parts[:PLANES, columns] = high
            parts[PLANES:, columns] = low
            return products + image * source[c]

        return jnp.sum(lax.fori_loop(0, NBE, column, jnp.zeros((PLANES, ED), F32)), axis=1, keepdims=True)

    def square_sum(left, right):
        total = jnp.zeros((PLANES, 1), F32)
        for t in range(TILES - 1):
            total = total + jnp.sum(left[t] * right[t], axis=1, keepdims=True)
        return total

    def put_dots(inst, rr, rw, ra):
        msg[inst, :, TILE:] = jnp.where(lane == 0, rr, jnp.where(lane == 1, rw, jnp.where(lane == 2, ra, 0.0)))

    msg[0, :, :TILE] = r8[TILES - 1]
    for t in range(TILES - 1):
        keep_parts(t, r8[t])
    dom_sum(0, 0, TILE, [lambda: gather_private(0, 5), lambda: gather_private(5, 10), lambda: gather_private(10, 16)])
    r_int = full[0, :, :TILE]
    r8[TILES - 1] = r_int
    gather_interface(r_int)

    gathered_r[...] = gathered_w[...]
    works = [
        lambda: assemble_private(0, 4),
        lambda: (assemble_private(4, 7), gather_private(0, 2)),
        lambda: gather_private(2, 16),
    ]

    norm = None
    energy = None
    alpha = None
    for step in range(3):
        inst = step + 1
        rw = operate(gathered_r)
        rr = square_sum(r8, r8)
        ra = square_sum(r8, a8) if step else jnp.zeros_like(rr)
        put_dots(inst, rr, rw, ra)
        if step < 2:
            msg[inst, :, :TILE] = assemble(TILES - 1)
            dom_sum(inst, 0, WIDE, works)
        else:
            dom_sum(inst, TILE, 128, [nothing] * 3)
        dots = full[inst, :, TILE:]
        r_int = r8[TILES - 1]
        rr = dots[:, 0:1] + jnp.sum(r_int * r_int, axis=1, keepdims=True)
        rw = dots[:, 1:2]
        if step:
            ra = dots[:, 2:3] + jnp.sum(r_int * a8[TILES - 1], axis=1, keepdims=True)
            beta = rr / norm
            energy = rw + 2.0 * beta * ra + beta * beta * energy
        else:
            energy = rw
        norm = rr
        alpha = norm / energy
        if step < 2:
            w_int = full[inst, :, :TILE]
            w8[TILES - 1] = w_int
            gather_interface(w_int)

            @pl.loop(0, NBE)
            def _(b):
                image = gathered_w[b]
                if step:
                    image = image + beta * gathered_a[b]
                if step < 1:
                    gathered_a[b] = image
                gathered_r[b] = gathered_r[b] - alpha * image

        for t in range(TILES):
            direction = r8[t]
            if step:
                direction = direction + beta * p8[t]
                iterate = x8[t] + alpha * direction
            else:
                iterate = alpha * direction
            if step < 2:
                p8[t] = direction
                x8[t] = iterate
                image = w8[t]
                if step:
                    image = image + beta * a8[t]
                a8[t] = image
                r8[t] = r8[t] - alpha * image
            elif t < TILES - 1:
                out_private[:, t * TILE:(t + 1) * TILE] = iterate
            else:
                out_interface[...] = iterate

    for copy in out_copies + back_copies:
        copy.wait_send()


def shards(velocity, gradient, project_table, jacobian, stiff_elem, mass_elem, bound_map):
    table = spanwise_table()
    high = table.astype(BF16)
    low = (table - high.astype(np.float32)).astype(BF16)
    vmem = pl.BlockSpec(memory_space=pltpu.VMEM)
    hbm = pl.BlockSpec(memory_space=pl.ANY)
    field = pltpu.VMEM((TILES, PLANES, TILE), F32)
    spread = pltpu.VMEM((NBE, PLANES, ED), F32)
    return pl.pallas_call(
        kernel,
        out_shape=(
            jax.ShapeDtypeStruct((PLANES, PRIV), F32),
            jax.ShapeDtypeStruct((PLANES, TILE), F32),
        ),
        in_specs=[hbm, hbm] + [vmem] * 6,
        out_specs=(vmem, vmem),
        scratch_shapes=[
            pltpu.VMEM((3, QP, PLANES, ED), BF16),
            pltpu.VMEM((3, QP, PLANES, ED), BF16),
            pltpu.VMEM((QP * PLANES, ED), F32),
            pltpu.VMEM((PLANES * NBE, ED), F32),
            pltpu.VMEM((TILES * TILE, NBE * ED), BF16),
            pltpu.VMEM((2 * PLANES, NBE * ED), BF16),
            pltpu.VMEM((2 * PLANES, TILES * TILE), BF16),
            spread, spread, spread,
            field, field, field, field, field, field,
            pltpu.VMEM((2, SIZE, TILE), F32),
            pltpu.VMEM((2, SIZE, TILE), F32),
            pltpu.VMEM((4, PLANES, WIDE), F32),
            pltpu.VMEM((4, GROUP, 8, WIDE), F32),
            pltpu.VMEM((4, GROUP, 8, WIDE), F32),
            pltpu.VMEM((4, PLANES, WIDE), F32),
            pltpu.SemaphoreType.DMA((2, QP // QCHUNK)),
            pltpu.SemaphoreType.DMA((2, SPAN)),
            pltpu.SemaphoreType.DMA((2, SPAN)),
            pltpu.SemaphoreType.DMA((4, 3, GROUP)),
            pltpu.SemaphoreType.DMA((4, 3, GROUP)),
        ],
        compiler_params=pltpu.CompilerParams(
            collective_id=0, has_side_effects=True, vmem_limit_bytes=56 * 1024 * 1024
        ),
    )(
        jnp.transpose(velocity, (0, 2, 1, 3)),
        jnp.transpose(gradient, (0, 2, 1, 3)),
        project_table.T,
        jacobian.reshape(1, ED),
        stiff_elem,
        mass_elem,
        bound_map,
        jnp.concatenate([jnp.asarray(high), jnp.asarray(low)], axis=0),
    )


def solution(mesh):
    return jax.shard_map(
        shards,
        mesh=mesh,
        in_specs=(
            P(None, "span", None, "dom"),
            P(None, "span", None, "dom"),
            P(),
            P("dom"),
            P(None, None, "dom"),
            P(None, None, "dom"),
            P(None, "dom"),
        ),
        out_specs=(P("span", "dom"), P("span", None)),
        check_vma=False,
    )
```

time: 1350 us -> 132 us (0.10)
  blocking collectives: 622 us -> 0 us
  waiting for transfers between devices: 400 us -> 0 us
  Pallas kernels: 0 us -> 128 us
  other arithmetic: 125 us -> 0 us
  local copies, waits for them, and re-layouts: 126 us -> 3.29 us
  matrix products: 41.6 us -> 0 us
  between operations: 14.5 us -> 0.64 us
    psum x5 -> x0, blocking collectives: 622 us -> none  [the longest x3 369 us: squares_of(): return lax.psum(own, 'dom') + shared]
    psum x4 -> x0, waiting for transfers between devices: 308 us -> none  [assemble(): shared = lax.psum(local[:, NB:], 'dom')]
    pallas_call x0 -> x1, Pallas kernels: none -> 128 us  [shards(): pl.pallas_call(kernel, out_shape=(jax.ShapeDtypeStruct((PLANES, PRIV), F3...]
    scatter-add x4 -> x0, other arithmetic: 94 us -> none  [assemble(): jnp.zeros((planes, NB + NIF), jnp.float32).at[:, flat]]
    all_to_all x2 -> x0, waiting for transfers between devices: 92.2 us -> none  [the longest x1 46.9 us: shards(): lax.all_to_all(forcing, 'span', split_axis=2, concat_axis=0, tiled=True)]
    gather x3 -> x0, local copies, waits for them, and re-layouts: 42.5 us -> none  [shards(): gathered = whole[:, bound_map]]
    dot_general x8 -> x0, matrix products: 41.6 us -> none  [the longest x3 15 us: shards(): first = jnp.einsum('cbe,mbe->mce', stiff_elem, gathered, precision=high)]
    unnamed x83 -> x2, local copies, waits for them, and re-layouts: 39 us -> 3.29 us
  transfers between devices with their start and end apart: 6 -> 0, of which waited for: 6 -> 0; matrix products, arithmetic and copies ran while one was open for 1% -> 0% of each run, Pallas kernels for 0% -> 0%
where the time goes in v1:
time: 132 us
  Pallas kernels  128 us (97%)
  local copies, waits for them, and re-layouts  3.29 us (2%)
    pallas_call x1, Pallas kernels, shards(): pl.pallas_call(kernel, out_shape=(jax.ShapeDtypeStruct((PLANES, PRIV), F3...  128 us
    unnamed x2, local copies, waits for them, and re-layouts  3.29 us

profile of v1, /device:TPU:1, one launch (start us, length us, event | category | flops | bytes accessed | tf_op | source)
XLA Modules:
  0.0 131.6 jit_solution(5818274113376301819)
XLA Ops:
  0.6 127.7 %shard_map.104 = (f32[64,1792]{1,0:T(8,128)}, f32[64,256]{1,0:T(8,128)}) custom-call(bf16[3,81,64,128]{3,2,1,0:T(8,128)(2,1)} %bitcast.4, bf16[3,81,64,128]{3,2,1,0:T(8,128)(2,1)} %bitcast.5, f32[32,81]{1,0:T(8,128)} %bitcast.6, f32[1,128]{1,0:T(1,128)} %bitcast.7, f32[32,32,128]{2,1,0:T(8,128)} %stiff.1, f32[32,32,128]{2,1,0:T(8,128)} %mass.1, ...), custom_call_target="tpu_custom_call" | custom-call | tf_op jit(solution)/shard_map/pallas_call | solution.py:368
  128.3 1.8 %copy.13 = f32[64,1792]{1,0:T(8,128)} copy(f32[64,1792]{1,0:T(8,128)} %get-tuple-element.4) | data formatting | bytes 917504
  130.1 1.5 %copy.14 = f32[64,256]{1,0:T(8,128)} copy(f32[64,256]{1,0:T(8,128)} %get-tuple-element.5) | data formatting | bytes 131072

commit v2 on v0

v2 whole, which is shorter than its diff:
```python
import jax
import jax.numpy as jnp
import numpy as np
from jax import lax
from jax.experimental import pallas as pl
from jax.experimental.pallas import tpu as pltpu
from jax.sharding import PartitionSpec as P

MESH = pl.DeviceIdType.MESH
F32 = jnp.float32
BF16 = jnp.bfloat16
QP = 81
NBE = 32
ED = 128
PLANES = 64
SIZE = 256
SPAN = 4
TILES = 8
TILE = 256
PRIV = 1792
GROUP = 8
WIDE = TILE + 128


def spanwise_table():
    index = np.arange(SIZE)
    kappa = np.where(index == 1, SIZE // 2, index // 2)
    angle = 2.0 * np.pi / SIZE * ((kappa[:, None] * index[None, :]) % SIZE)
    scale = np.where(index < 2, np.sqrt(1.0 / SIZE), np.sqrt(2.0 / SIZE))
    odd = (index % 2 == 1) & (index != 1)
    return (np.where(odd[:, None], -np.sin(angle), np.cos(angle)) * scale[:, None]).astype(np.float32)


def split(values):
    high = values.astype(BF16)
    return high, (values - high.astype(F32)).astype(BF16)


def both(product):
    half = product.shape[0] // 2
    return product[:half] + product[half:]


def dot(left, right):
    return jnp.dot(left, right, preferred_element_type=F32)


def kernel(
    vel_hbm, grad_hbm, project, jacobian, bmap, stiff_hbm, mass_hbm, table_hbm, wrap_hbm,
    out,
    stiff, mass, table, wrap, cols, rows_hot, shifted, parts, vparts, gathered_w, gathered_a, gathered_r,
    w8, a8, p8, r8, x8, cross, modes, interface,
    msg, recv_a, recv_b, full, dots_a, dots_b, factors, state,
    in_sem, span_send, span_recv, dom_send, dom_recv,
):
    s = lax.axis_index("span")
    d = lax.axis_index("dom")
    zi = lax.div(d, GROUP)
    i = lax.rem(d, GROUP)

    chunks = [(0, 32), (32, 32), (64, QP - 64)]

    def chunk_copies(index):
        start, count = chunks[index]
        copies = []
        for which, source in enumerate((vel_hbm, grad_hbm)):
            for c in range(3):
                slab = which * 9 + c * 3 + index
                copies.append(pltpu.make_async_copy(
                    source.at[c, pl.ds(start * PLANES, count * PLANES)],
                    cols.at[slab, pl.ds(0, count * PLANES)],
                    in_sem.at[slab],
                ))
        return copies

    for index in range(3):
        for copy in chunk_copies(index):
            copy.start()

    small_copies = [
        pltpu.make_async_copy(src, dst, in_sem.at[18 + k])
        for k, (src, dst) in enumerate(((stiff_hbm, stiff), (mass_hbm, mass), (table_hbm, table), (wrap_hbm, wrap)))
    ]
    for copy in small_copies:
        copy.start()

    barrier = pltpu.get_barrier_semaphore()
    def start(copies):
        first, last, make = copies

        @pl.loop(first, last)
        def _(k):
            make(k).start()

        return copies

    def arrive(copies):
        first, last, make = copies

        @pl.loop(first, last)
        def _(k):
            make(k).wait_recv()

    def leave(*groups):
        for first, last, make in groups:
            @pl.loop(first, last)
            def _(k, make=make):
                make(k).wait_send()

    def same_z(k):
        return zi * GROUP + lax.rem(i + k, GROUP)

    def along_z(k):
        return lax.rem(zi + k, GROUP) * GROUP + i

    @pl.loop(1, GROUP)
    def _(k):
        pl.semaphore_signal(barrier, inc=1, device_id=(s, same_z(k)), device_id_type=MESH)
        pl.semaphore_signal(barrier, inc=1, device_id=(s, along_z(k)), device_id_type=MESH)

    @pl.loop(1, SPAN)
    def _(k):
        pl.semaphore_signal(barrier, inc=1, device_id=(lax.rem(s + k, SPAN), d), device_id_type=MESH)

    @pl.loop(0, NBE, unroll=2)
    def _(b):
        here = jnp.transpose(jnp.broadcast_to(bmap[pl.ds(b, 1), :], (ED, ED)))
        lane = lax.broadcasted_iota(jnp.int32, (16, ED), 1)
        for r in range(0, ED, 16):
            tile = lax.shift_right_logical(here[r:r + 16], 7).astype(F32).astype(BF16)
            hot = jnp.where((here[r:r + 16] & (ED - 1)) == lane, 1.0, 0.0).astype(BF16)
            for j in range(TILES * TILE // ED):
                rows_hot[pl.ds(pl.multiple_of(b * ED + r, 16), 16), j * ED:(j + 1) * ED] = jnp.where(
                    tile == jnp.bfloat16(j), hot, jnp.zeros_like(hot)
                )

    for index in range(3):
        for copy in chunk_copies(index):
            copy.wait()

        @pl.loop(0, chunks[index][1])
        def _(q, index=index):
            here = pl.ds(pl.multiple_of(q * PLANES, PLANES), PLANES)

            def value(which, c):
                return cols[which * 9 + c * 3 + index, here].astype(F32)

            first = value(0, 0)
            advect = first * value(1, 0) + value(0, 1) * value(1, 1) + value(0, 2) * value(1, 2)
            row = pl.multiple_of((q + chunks[index][0]) * PLANES, PLANES)
            shifted[pl.ds(row, PLANES), :] = first - 0.5 * advect

    project_high, project_low = split(project[...])
    project_both = jnp.concatenate([project_high, project_low], axis=0)
    area = jnp.concatenate([jacobian[...], jacobian[...]], axis=1)
    loads = QP * PLANES

    @pl.loop(0, PLANES // 2, unroll=4)
    def _(pair):
        values = jnp.concatenate(
            [shifted[pl.ds(2 * pair + k, QP, stride=PLANES), :] for k in range(2)], axis=1
        )
        high, low = split(values)
        load = (both(dot(project_both, high)) + dot(project_high, low)) * area
        start = pl.multiple_of(loads + pair * 2 * NBE, 2 * NBE)
        shifted[pl.ds(start, NBE), :] = load[:, :ED]
        shifted[pl.ds(start + NBE, NBE), :] = load[:, ED:]

    @pl.loop(0, NBE, unroll=4)
    def _(b):
        high, low = split(shifted[pl.ds(loads + b, PLANES, stride=NBE), :])
        columns = pl.ds(pl.multiple_of(b * ED, ED), ED)
        parts[:PLANES, columns] = high
        parts[PLANES:, columns] = low

    def remote(inst, stage, k, src, dst, target):
        return pltpu.make_async_remote_copy(
            src_ref=src, dst_ref=dst, send_sem=dom_send.at[inst, stage, k], recv_sem=dom_recv.at[inst, stage, k],
            device_id=(s, target), device_id_type=MESH,
        )

    def across(stage, k, src, dst):
        return pltpu.make_async_remote_copy(
            src_ref=src, dst_ref=dst, send_sem=span_send.at[stage, k], recv_sem=span_recv.at[stage, k],
            device_id=(lax.rem(s + k, SPAN), d), device_id_type=MESH,
        )

    def rows_of(index):
        return pl.ds(pl.multiple_of(index * 8, 8), 8)

    def scatter_sum(inst, columns):
        def make(k):
            peer = lax.rem(i + k, GROUP)
            return remote(
                inst, 0, k, msg.at[inst, rows_of(peer), columns], recv_a.at[inst, k, :, columns], zi * GROUP + peer
            )

        return start((1, GROUP, make))

    def depth_sum(inst, columns):
        total = msg[inst, rows_of(i), columns]
        for k in range(1, GROUP):
            total = total + recv_a[inst, k, :, columns]
        recv_b[inst, zi, :, columns] = total
        own = recv_b.at[inst, zi, :, columns]
        return start((1, GROUP, lambda k: remote(inst, 1, k, own, own, along_z(k))))

    def depth_total(inst, columns):
        total = recv_b[inst, 0, :, columns]
        for k in range(1, GROUP):
            total = total + recv_b[inst, k, :, columns]
        return total

    def within(inst, stage, own):
        return start((1, GROUP, lambda k: remote(inst, stage, k, own, own, same_z(k))))

    def assemble(first, count):
        return both(dot(parts[...], rows_hot[:, first * TILE:(first + count) * TILE]))

    shared = pl.ds(0, TILE)
    msg[0, :, shared] = assemble(TILES - 1, 1)
    pl.semaphore_wait(barrier, 2 * (GROUP - 1) + SPAN - 1)
    int_a = scatter_sum(0, shared)
    rows = pl.ds(pl.multiple_of(s * PLANES, PLANES), PLANES)

    def out_copy(k):
        return across(0, k, w8.at[pl.ds(2 * lax.rem(s + k, SPAN), 2)], cross.at[:, rows])

    @pl.loop(1, SPAN + 1)
    def _(k):
        j = lax.rem(s + k, SPAN)
        chunk = both(dot(parts[...], rows_hot[:, pl.ds(pl.multiple_of(j * 2 * TILE, 2 * TILE), 2 * TILE)]))
        for half in range(2):
            w8[2 * j + half] = chunk[:, half * TILE:(half + 1) * TILE]

        @pl.when(k < SPAN)
        def _():
            out_copy(k).start()

    out_copies = (1, SPAN, out_copy)
    cross[:, rows, :] = w8[pl.ds(2 * s, 2)]
    arrive(int_a)
    int_b = depth_sum(0, shared)

    for copy in small_copies:
        copy.wait()
    wave = (lax.broadcasted_iota(jnp.int32, (PLANES // 2, ED), 0) + s * (PLANES // 2)).astype(F32) * (1.0 / SIZE)
    shift = 0.5 + 8.0 * wave * wave

    @pl.loop(0, NBE)
    def _(c):
        for b in range(NBE):
            row = pl.multiple_of((c * NBE + b) * (PLANES // 2), PLANES // 2)
            shifted[pl.ds(row, PLANES // 2), :] = stiff[c, pl.ds(b, 1), :] + shift * mass[c, pl.ds(b, 1), :]

    arrive(out_copies)

    @pl.loop(0, 2)
    def _(half):
        high, low = split(cross[half])
        modes[half] = both(dot(table[...], high)) + dot(table[:SIZE, :], low)

    def back_copy(k):
        there = pl.ds(pl.multiple_of(lax.rem(s + k, SPAN) * PLANES, PLANES), PLANES)
        return across(1, k, modes.at[:, there], r8.at[pl.ds(2 * s, 2)])

    back_copies = start((1, SPAN, back_copy))
    r8[pl.ds(2 * s, 2)] = modes[:, pl.ds(pl.multiple_of(s * PLANES, PLANES), PLANES), :]

    arrive(int_b)
    interface[i, s] = depth_total(0, shared)
    int_c = start((1, SPAN, lambda k: across(2, k, interface.at[i, s], interface.at[i, s])))

    @pl.loop(0, NBE)
    def _(b):
        here = jnp.broadcast_to(bmap[pl.ds(b, 1), :], (16, ED))
        row = lax.broadcasted_iota(jnp.int32, (16, ED), 0)
        tile = lax.shift_right_logical(here, 4).astype(F32).astype(BF16)
        hot = jnp.where((here & 15) == row, 1.0, 0.0).astype(BF16)
        for g in range(TILES * TILE // 16):
            cols[b, pl.ds(g * 16, 16), :] = jnp.where(tile == jnp.bfloat16(g), hot, jnp.zeros_like(hot))

    arrive(int_c)
    int_d = within(0, 2, interface.at[i])
    for field in (a8, p8, x8, gathered_a):
        field[...] = jnp.zeros_like(field)

    def keep_parts(tile, values):
        high, low = split(values)
        columns = pl.ds(pl.multiple_of(tile * TILE, TILE), TILE)
        vparts[:PLANES, columns] = high
        vparts[PLANES:, columns] = low

    def gather_private(target):
        @pl.loop(0, 4)
        def _(n):
            hot = jnp.concatenate([cols[n * 8 + k, :PRIV] for k in range(8)], axis=1)
            out = both(dot(vparts[:, :PRIV], hot))
            for k in range(8):
                target[8 * n + k] = out[:, k * ED:(k + 1) * ED]

    def gather_interface(target, values):
        high, low = split(values)
        rest = (values - high.astype(F32) - low.astype(F32)).astype(BF16)
        lhs = jnp.concatenate([high, low, rest], axis=0)
        for n in range(4):
            hot = jnp.concatenate([cols[n * 8 + k, PRIV:] for k in range(8)], axis=1)
            out = dot(lhs, hot)
            out = out[:PLANES] + out[PLANES:2 * PLANES] + out[2 * PLANES:]
            for k in range(8):
                target[8 * n + k] += out[:, k * ED:(k + 1) * ED]

    leave(out_copies)
    arrive(back_copies)

    @pl.loop(0, TILES - 1)
    def _(t):
        keep_parts(t, r8[t])

    gather_private(gathered_r)
    arrive(int_d)
    high, low = split(interface[...].reshape(SIZE, TILE))
    wrap_high = wrap[pl.ds(pl.multiple_of(s * PLANES, PLANES), PLANES), :]
    wrap_low = wrap[pl.ds(pl.multiple_of(SIZE + s * PLANES, PLANES), PLANES), :]
    r_int = dot(wrap_high, high) + dot(wrap_low, high) + dot(wrap_high, low)
    r8[TILES - 1] = r_int
    gather_interface(gathered_r, r_int)
    leave(int_a, int_b, int_c, int_d, back_copies)

    def dom_sum(inst):
        columns = pl.ds(0, WIDE)
        first = scatter_sum(inst, columns)
        assemble_private()
        arrive(first)
        second = depth_sum(inst, columns)
        gather_private(gathered_w)
        arrive(second)
        full[inst, rows_of(i), columns] = depth_total(inst, columns)
        third = within(inst, 2, full.at[inst, rows_of(i), columns])
        arrive(third)
        leave(first, second, third)

    def dots_sum(values):
        square = jnp.concatenate([values, jnp.zeros_like(values)], axis=0)
        dots_a[i] = jnp.transpose(square)[:8]
        first = within(0, 3, dots_a.at[i])
        arrive(first)
        total = dots_a[0]
        for k in range(1, GROUP):
            total = total + dots_a[k]
        dots_b[zi] = total
        own = dots_b.at[zi]
        second = start((1, GROUP, lambda k: remote(1, 3, k, own, own, along_z(k))))
        arrive(second)
        total = dots_b[0]
        for k in range(1, GROUP):
            total = total + dots_b[k]
        leave(first, second)
        square = jnp.concatenate([total, jnp.zeros((ED - 8, ED), F32)], axis=0)
        return jnp.transpose(square)[:PLANES]

    def assemble_private():
        @pl.loop(0, TILES // 2)
        def _(pair):
            columns = pl.ds(pl.multiple_of(pair * 2 * TILE, 2 * TILE), 2 * TILE)
            out = both(dot(parts[...], rows_hot[:, columns]))
            for half in range(2):
                values = out[:, half * TILE:(half + 1) * TILE]
                w8[2 * pair + half] = values
                keep_parts(2 * pair + half, values)

    lane = lax.broadcasted_iota(jnp.int32, (PLANES, ED), 1)
    extra = jnp.where(s == 0, 2.0, 0.0)
    top = lax.broadcasted_iota(jnp.int32, (PLANES // 2, ED), 0) == 0
    half_rows = PLANES // 2
    block = 4

    def operate(source):
        special = source[:, half_rows, :] * extra

        @pl.loop(0, NBE // block)
        def _(step):
            sums = [[jnp.zeros((half_rows, ED), F32) for _ in range(2)] for _ in range(block)]
            for b in range(NBE):
                even = source[b, :half_rows]
                odd = source[b, half_rows:]
                for k in range(block):
                    row = pl.multiple_of(((step * block + k) * NBE + b) * half_rows, half_rows)
                    matrix = shifted[pl.ds(row, half_rows), :]
                    sums[k][0] = sums[k][0] + matrix * even
                    sums[k][1] = sums[k][1] + matrix * odd
            for k in range(block):
                gathered_w[step * block + k, :half_rows] = sums[k][0]
                gathered_w[step * block + k, half_rows:] = sums[k][1]

        def column(c, products):
            fix = jnp.sum(mass[c] * special, axis=0, keepdims=True)
            image = jnp.concatenate(
                [gathered_w[c, :half_rows], gathered_w[c, half_rows:] + jnp.where(top, fix, 0.0)], axis=0
            )
            high, low = split(image)
            columns = pl.ds(pl.multiple_of(c * ED, ED), ED)
            parts[:PLANES, columns] = high
            parts[PLANES:, columns] = low
            return products + image * source[c]

        products = lax.fori_loop(0, NBE, column, jnp.zeros((PLANES, ED), F32), unroll=4)
        return jnp.sum(products, axis=1, keepdims=True)

    def product_sum(left, right):
        total = left[0] * right[0]
        for t in range(1, TILES - 1):
            total = total + left[t] * right[t]
        return jnp.sum(total, axis=1, keepdims=True)

    state[0] = jnp.ones((PLANES, ED), F32)
    state[1] = jnp.zeros((PLANES, ED), F32)

    @pl.loop(0, 3)
    def _(step):
        rw = operate(gathered_r)
        rr = product_sum(r8, r8)
        ra = product_sum(r8, a8)
        own = jnp.where(lane == 0, rr, jnp.where(lane == 1, rw, jnp.where(lane == 2, ra, 0.0)))

        @pl.when(step < 2)
        def _():
            msg[step + 1, :, :TILE] = assemble(TILES - 1, 1)
            msg[step + 1, :, TILE:] = own
            dom_sum(step + 1)
            state[2] = full[step + 1, :, TILE:]

        @pl.when(step == 2)
        def _():
            state[2] = dots_sum(own)

        r_int = r8[TILES - 1]
        rr = state[2, :, 0:1] + jnp.sum(r_int * r_int, axis=1, keepdims=True)
        rw = state[2, :, 1:2]
        ra = state[2, :, 2:3] + jnp.sum(r_int * a8[TILES - 1], axis=1, keepdims=True)
        beta = jnp.where(step == 0, 0.0, rr / state[0, :, 0:1])
        energy = rw + 2.0 * beta * ra + beta * beta * state[1, :, 0:1]
        state[0] = jnp.broadcast_to(rr, (PLANES, ED))
        state[1] = jnp.broadcast_to(energy, (PLANES, ED))
        factors[0] = jnp.broadcast_to(rr / energy, (PLANES, TILE))
        factors[1] = jnp.broadcast_to(beta, (PLANES, TILE))

        @pl.when(step < 2)
        def _():
            w_int = full[step + 1, :, :TILE]
            w8[TILES - 1] = w_int
            gather_interface(gathered_w, w_int)

            @pl.loop(0, NBE, unroll=2)
            def _(b):
                image = gathered_w[b] + factors[1, :, :ED] * gathered_a[b]
                gathered_a[b] = image
                gathered_r[b] = gathered_r[b] - factors[0, :, :ED] * image

        @pl.loop(0, TILES)
        def _(t):
            direction = r8[t] + factors[1] * p8[t]
            p8[t] = direction
            x8[t] = x8[t] + factors[0] * direction
            image = w8[t] + factors[1] * a8[t]
            a8[t] = image
            r8[t] = r8[t] - factors[0] * image

    @pl.loop(0, TILES)
    def _(t):
        for part in range(2):
            slab = out.at[2 * t + part]
            for parity in range(2):
                mine = x8[t, parity * half_rows:(parity + 1) * half_rows, part * ED:(part + 1) * ED]
                slab[pl.ds(parity, half_rows, stride=2), :] = mine


def place(slabs, out_private, out_interface):
    for n in range(TILES * TILE // ED):
        if n < PRIV // ED:
            out_private[:, n * ED:(n + 1) * ED] = slabs[n]
        else:
            out_interface[:, n * ED - PRIV:(n + 1) * ED - PRIV] = slabs[n]


def shards(velocity, gradient, project_table, jacobian, stiff_elem, mass_elem, bound_map):
    order = np.arange(SIZE).reshape(SPAN, PLANES // 2, 2).transpose(0, 2, 1).reshape(-1)
    table = spanwise_table()[order]
    wrap = table[:, np.arange(SIZE).reshape(SPAN, GROUP, 8).transpose(1, 0, 2).reshape(-1)]

    def in_parts(values):
        high = values.astype(BF16)
        return jnp.asarray(np.concatenate([high, (values - high.astype(np.float32)).astype(BF16)], axis=0))

    vmem = pl.BlockSpec(memory_space=pltpu.VMEM)
    hbm = pl.BlockSpec(memory_space=pl.ANY)
    field = pltpu.VMEM((TILES, PLANES, TILE), F32)
    spread = pltpu.VMEM((NBE, PLANES, ED), F32)
    slabs = pl.pallas_call(
        kernel,
        out_shape=jax.ShapeDtypeStruct((TILES * TILE // ED, PLANES, ED), F32),
        in_specs=[hbm, hbm] + [vmem] * 3 + [hbm] * 4,
        out_specs=vmem,
        scratch_shapes=[
            pltpu.VMEM((NBE, NBE, ED), F32),
            pltpu.VMEM((NBE, NBE, ED), F32),
            pltpu.VMEM((2 * SIZE, SIZE), BF16),
            pltpu.VMEM((2 * SIZE, SIZE), BF16),
            pltpu.VMEM((NBE, TILES * TILE, ED), BF16),
            pltpu.VMEM((NBE * ED, TILES * TILE), BF16),
            pltpu.VMEM((NBE * NBE * PLANES // 2, ED), F32),
            pltpu.VMEM((2 * PLANES, NBE * ED), BF16),
            pltpu.VMEM((2 * PLANES, TILES * TILE), BF16),
            spread, spread, spread,
            field, field, field, field, field,
            pltpu.VMEM((2, SIZE, TILE), F32),
            pltpu.VMEM((2, SIZE, TILE), F32),
            pltpu.VMEM((GROUP, SPAN, 8, TILE), F32),
            pltpu.VMEM((3, PLANES, WIDE), F32),
            pltpu.VMEM((3, GROUP, 8, WIDE), F32),
            pltpu.VMEM((3, GROUP, 8, WIDE), F32),
            pltpu.VMEM((3, PLANES, WIDE), F32),
            pltpu.VMEM((GROUP, 8, ED), F32),
            pltpu.VMEM((GROUP, 8, ED), F32),
            pltpu.VMEM((2, PLANES, TILE), F32),
            pltpu.VMEM((3, PLANES, ED), F32),
            pltpu.SemaphoreType.DMA((22,)),
            pltpu.SemaphoreType.DMA((3, SPAN)),
            pltpu.SemaphoreType.DMA((3, SPAN)),
            pltpu.SemaphoreType.DMA((3, 4, GROUP)),
            pltpu.SemaphoreType.DMA((3, 4, GROUP)),
        ],
        compiler_params=pltpu.CompilerParams(
            collective_id=0, has_side_effects=True, vmem_limit_bytes=62 * 1024 * 1024
        ),
    )(
        jnp.transpose(velocity, (0, 2, 1, 3)).reshape(3, QP * PLANES, ED),
        jnp.transpose(gradient, (0, 2, 1, 3)).reshape(3, QP * PLANES, ED),
        project_table.T,
        jacobian.reshape(1, ED),
        bound_map,
        stiff_elem,
        mass_elem,
        in_parts(table),
        in_parts(wrap),
    )
    return pl.pallas_call(
        place,
        out_shape=(jax.ShapeDtypeStruct((PLANES, PRIV), F32), jax.ShapeDtypeStruct((PLANES, TILE), F32)),
        in_specs=[vmem],
        out_specs=(vmem, vmem),
    )(slabs)


def solution(mesh):
    return jax.shard_map(
        shards,
        mesh=mesh,
        in_specs=(
            P(None, "span", None, "dom"),
            P(None, "span", None, "dom"),
            P(),
            P("dom"),
            P(None, None, "dom"),
            P(None, None, "dom"),
            P(None, "dom"),
        ),
        out_specs=(P("span", "dom"), P("span", None)),
        check_vma=False,
    )
```

time: 1350 us -> 102 us (0.08)
  blocking collectives: 622 us -> 0 us
  waiting for transfers between devices: 400 us -> 0 us
  local copies, waits for them, and re-layouts: 126 us -> 0 us
  other arithmetic: 125 us -> 0 us
  Pallas kernels: 0 us -> 101 us
  matrix products: 41.6 us -> 0 us
  between operations: 14.5 us -> 0.64 us
    psum x5 -> x0, blocking collectives: 622 us -> none  [the longest x3 369 us: squares_of(): return lax.psum(own, 'dom') + shared]
    psum x4 -> x0, waiting for transfers between devices: 308 us -> none  [assemble(): shared = lax.psum(local[:, NB:], 'dom')]
    pallas_call x0 -> x2, Pallas kernels: none -> 101 us  [the longest x1 99 us: shards(): pl.pallas_call(kernel, out_shape=jax.ShapeDtypeStruct((TILES * TILE // ED...]
    scatter-add x4 -> x0, other arithmetic: 94 us -> none  [assemble(): jnp.zeros((planes, NB + NIF), jnp.float32).at[:, flat]]
    all_to_all x2 -> x0, waiting for transfers between devices: 92.2 us -> none  [the longest x1 46.9 us: shards(): lax.all_to_all(forcing, 'span', split_axis=2, concat_axis=0, tiled=True)]
    gather x3 -> x0, local copies, waits for them, and re-layouts: 42.5 us -> none  [shards(): gathered = whole[:, bound_map]]
    dot_general x8 -> x0, matrix products: 41.6 us -> none  [the longest x3 15 us: shards(): first = jnp.einsum('cbe,mbe->mce', stiff_elem, gathered, precision=high)]
    unnamed x83 -> x0, local copies, waits for them, and re-layouts: 39 us -> none
  transfers between devices with their start and end apart: 6 -> 0, of which waited for: 6 -> 0; matrix products, arithmetic and copies ran while one was open for 1% -> 0% of each run, Pallas kernels for 0% -> 0%
where the time goes in v2:
time: 102 us; the launch traced here: 101 us
  Pallas kernels  101 us (99%)
    pallas_call x1, Pallas kernels, shards(): pl.pallas_call(kernel, out_shape=jax.ShapeDtypeStruct((TILES * TILE // ED...  99 us

profile of v2, /device:TPU:1, one launch (start us, length us, event | category | flops | bytes accessed | tf_op | source)
XLA Modules:
  0.0 101.5 jit_solution(13999616489720405926)
XLA Ops:
  0.6 99.0 %shard_map.104.slabs = f32[16,64,128]{2,1,0:T(8,128)} custom-call(bf16[3,5184,128]{2,1,0:T(8,128)(2,1)} %bitcast.8, bf16[3,5184,128]{2,1,0:T(8,128)(2,1)} %bitcast.9, f32[32,81]{1,0:T(8,128)} %bitcast.10, f32[1,128]{1,0:T(1,128)} %bitcast.11, s32[32,128]{1,0:T(8,128)} %bmap.1, f32[32,32,128]{2,1,0:T(8,128)} %stiff_hbm.1, f32[32,32,128]{2,1,0:T(8,128)} %mass_hbm.1, ...), custom_call_target="tpu_custom_call" | custom-call | tf_op jit(solution)/shard_map/pallas_call | solution.py:499
  99.6 1.9 %shard_map.105 = (f32[64,1792]{1,0:T(8,128)}, f32[64,256]{1,0:T(8,128)}) custom-call(f32[16,64,128]{2,1,0:T(8,128)} %shard_map.104.slabs), custom_call_target="tpu_custom_call" | custom-call | tf_op jit(solution)/shard_map/pallas_call | solution.py:547

commit v3 on v2

--- a/solution.py
+++ b/solution.py
@@ -19,7 +19,6 @@
 TILE = 256
 PRIV = 1792
 GROUP = 8
-WIDE = TILE + 128
 
 
 def spanwise_table():
@@ -122,9 +121,11 @@
     def _(k):
         pl.semaphore_signal(barrier, inc=1, device_id=(lax.rem(s + k, SPAN), d), device_id_type=MESH)
 
-    @pl.loop(0, NBE, unroll=2)
-    def _(b):
-        here = jnp.transpose(jnp.broadcast_to(bmap[pl.ds(b, 1), :], (ED, ED)))
+    def turned(b):
+        return jnp.transpose(jnp.broadcast_to(bmap[pl.ds(b, 1), :], (ED, ED)))
+
+    def hot_rows(b, here):
+        following = turned(lax.rem(b + 1, NBE))
         lane = lax.broadcasted_iota(jnp.int32, (16, ED), 1)
         for r in range(0, ED, 16):
             tile = lax.shift_right_logical(here[r:r + 16], 7).astype(F32).astype(BF16)
@@ -133,6 +134,9 @@
                 rows_hot[pl.ds(pl.multiple_of(b * ED + r, 16), 16), j * ED:(j + 1) * ED] = jnp.where(
                     tile == jnp.bfloat16(j), hot, jnp.zeros_like(hot)
                 )
+        return following
+
+    lax.fori_loop(0, NBE, hot_rows, turned(0))
 
     for index in range(3):
         for copy in chunk_copies(index):
@@ -188,27 +192,35 @@
     def rows_of(index):
         return pl.ds(pl.multiple_of(index * 8, 8), 8)
 
-    def scatter_sum(inst, columns):
+    def scatter_copies(inst):
         def make(k):
             peer = lax.rem(i + k, GROUP)
-            return remote(
-                inst, 0, k, msg.at[inst, rows_of(peer), columns], recv_a.at[inst, k, :, columns], zi * GROUP + peer
-            )
-
-        return start((1, GROUP, make))
-
-    def depth_sum(inst, columns):
-        total = msg[inst, rows_of(i), columns]
+            return remote(inst, 0, k, msg.at[inst, rows_of(peer)], recv_a.at[inst, k], zi * GROUP + peer)
+
+        return 1, GROUP, make
+
+    def depth_copies(inst):
+        own = recv_b.at[inst, zi]
+        return 1, GROUP, lambda k: remote(inst, 1, k, own, own, along_z(k))
+
+    def share_copies(inst):
+        own = full.at[inst, rows_of(i)]
+        return 1, GROUP, lambda k: remote(inst, 2, k, own, own, same_z(k))
+
+    def scatter_sum(inst):
+        return start(scatter_copies(inst))
+
+    def depth_sum(inst):
+        total = msg[inst, rows_of(i)]
         for k in range(1, GROUP):
-            total = total + recv_a[inst, k, :, columns]
-        recv_b[inst, zi, :, columns] = total
-        own = recv_b.at[inst, zi, :, columns]
-        return start((1, GROUP, lambda k: remote(inst, 1, k, own, own, along_z(k))))
-
-    def depth_total(inst, columns):
-        total = recv_b[inst, 0, :, columns]
+            total = total + recv_a[inst, k]
+        recv_b[inst, zi] = total
+        return start(depth_copies(inst))
+
+    def depth_total(inst):
+        total = recv_b[inst, 0]
         for k in range(1, GROUP):
-            total = total + recv_b[inst, k, :, columns]
+            total = total + recv_b[inst, k]
         return total
 
     def within(inst, stage, own):
@@ -217,10 +229,9 @@
     def assemble(first, count):
         return both(dot(parts[...], rows_hot[:, first * TILE:(first + count) * TILE]))
 
-    shared = pl.ds(0, TILE)
-    msg[0, :, shared] = assemble(TILES - 1, 1)
+    msg[0] = assemble(TILES - 1, 1)
     pl.semaphore_wait(barrier, 2 * (GROUP - 1) + SPAN - 1)
-    int_a = scatter_sum(0, shared)
+    int_a = scatter_sum(0)
     rows = pl.ds(pl.multiple_of(s * PLANES, PLANES), PLANES)
 
     def out_copy(k):
@@ -240,7 +251,7 @@
     out_copies = (1, SPAN, out_copy)
     cross[:, rows, :] = w8[pl.ds(2 * s, 2)]
     arrive(int_a)
-    int_b = depth_sum(0, shared)
+    int_b = depth_sum(0)
 
     for copy in small_copies:
         copy.wait()
@@ -268,7 +279,7 @@
     r8[pl.ds(2 * s, 2)] = modes[:, pl.ds(pl.multiple_of(s * PLANES, PLANES), PLANES), :]
 
     arrive(int_b)
-    interface[i, s] = depth_total(0, shared)
+    interface[i, s] = depth_total(0)
     int_c = start((1, SPAN, lambda k: across(2, k, interface.at[i, s], interface.at[i, s])))
 
     @pl.loop(0, NBE)
@@ -282,7 +293,7 @@
 
     arrive(int_c)
     int_d = within(0, 2, interface.at[i])
-    for field in (a8, p8, x8, gathered_a):
+    for field in (a8, p8, x8, gathered_a, gathered_r):
         field[...] = jnp.zeros_like(field)
 
     def keep_parts(tile, values):
@@ -299,7 +310,7 @@
             for k in range(8):
                 target[8 * n + k] = out[:, k * ED:(k + 1) * ED]
 
-    def gather_interface(target, values):
+    def gather_interface(add, values):
         high, low = split(values)
         rest = (values - high.astype(F32) - low.astype(F32)).astype(BF16)
         lhs = jnp.concatenate([high, low, rest], axis=0)
@@ -308,56 +319,42 @@
             out = dot(lhs, hot)
             out = out[:PLANES] + out[PLANES:2 * PLANES] + out[2 * PLANES:]
             for k in range(8):
-                target[8 * n + k] += out[:, k * ED:(k + 1) * ED]
+                add(8 * n + k, out[:, k * ED:(k + 1) * ED])
 
     leave(out_copies)
-    arrive(back_copies)
-
-    @pl.loop(0, TILES - 1)
-    def _(t):
-        keep_parts(t, r8[t])
-
-    gather_private(gathered_r)
+
+    @pl.loop(0, SPAN)
+    def _(turn):
+        k = turn + turn // 2 - 2 * (turn // 3)
+        j = lax.rem(s + SPAN - k, SPAN)
+
+        @pl.when(turn > 0)
+        def _():
+            back_copy(k).wait_recv()
+
+        for half in range(2):
+            keep_parts(2 * j + half, jnp.where(2 * j + half < TILES - 1, r8[2 * j + half], 0.0))
+        chunk = pl.ds(pl.multiple_of(j * 2 * TILE, 2 * TILE), 2 * TILE)
+
+        @pl.loop(0, 4)
+        def _(n):
+            hot = jnp.concatenate([cols[n * 8 + m, chunk] for m in range(8)], axis=1)
+            out = both(dot(vparts[:, chunk], hot))
+            for m in range(8):
+                gathered_r[8 * n + m] += out[:, m * ED:(m + 1) * ED]
+
     arrive(int_d)
     high, low = split(interface[...].reshape(SIZE, TILE))
     wrap_high = wrap[pl.ds(pl.multiple_of(s * PLANES, PLANES), PLANES), :]
     wrap_low = wrap[pl.ds(pl.multiple_of(SIZE + s * PLANES, PLANES), PLANES), :]
     r_int = dot(wrap_high, high) + dot(wrap_low, high) + dot(wrap_high, low)
     r8[TILES - 1] = r_int
-    gather_interface(gathered_r, r_int)
+
+    def add_first(b, values):
+        gathered_r[b] += values
+
+    gather_interface(add_first, r_int)
     leave(int_a, int_b, int_c, int_d, back_copies)
-
-    def dom_sum(inst):
-        columns = pl.ds(0, WIDE)
-        first = scatter_sum(inst, columns)
-        assemble_private()
-        arrive(first)
-        second = depth_sum(inst, columns)
-        gather_private(gathered_w)
-        arrive(second)
-        full[inst, rows_of(i), columns] = depth_total(inst, columns)
-        third = within(inst, 2, full.at[inst, rows_of(i), columns])
-        arrive(third)
-        leave(first, second, third)
-
-    def dots_sum(values):
-        square = jnp.concatenate([values, jnp.zeros_like(values)], axis=0)
-        dots_a[i] = jnp.transpose(square)[:8]
-        first = within(0, 3, dots_a.at[i])
-        arrive(first)
-        total = dots_a[0]
-        for k in range(1, GROUP):
-            total = total + dots_a[k]
-        dots_b[zi] = total
-        own = dots_b.at[zi]
-        second = start((1, GROUP, lambda k: remote(1, 3, k, own, own, along_z(k))))
-        arrive(second)
-        total = dots_b[0]
-        for k in range(1, GROUP):
-            total = total + dots_b[k]
-        leave(first, second)
-        square = jnp.concatenate([total, jnp.zeros((ED - 8, ED), F32)], axis=0)
-        return jnp.transpose(square)[:PLANES]
 
     def assemble_private():
         @pl.loop(0, TILES // 2)
@@ -423,21 +420,43 @@
         ra = product_sum(r8, a8)
         own = jnp.where(lane == 0, rr, jnp.where(lane == 1, rw, jnp.where(lane == 2, ra, 0.0)))
 
+        inst = step + 1
+        dots_a[step, i] = jnp.transpose(jnp.concatenate([own, jnp.zeros_like(own)], axis=0))[:8]
+        dots_first = within(inst, 3, dots_a.at[step, i])
+
         @pl.when(step < 2)
         def _():
-            msg[step + 1, :, :TILE] = assemble(TILES - 1, 1)
-            msg[step + 1, :, TILE:] = own
-            dom_sum(step + 1)
-            state[2] = full[step + 1, :, TILE:]
-
-        @pl.when(step == 2)
+            msg[inst] = assemble(TILES - 1, 1)
+            scatter_sum(inst)
+            assemble_private()
+
+        arrive(dots_first)
+        total = dots_a[step, 0]
+        for k in range(1, GROUP):
+            total = total + dots_a[step, k]
+        dots_b[step, zi] = total
+        dots_second = start((1, GROUP, lambda k: remote(
+            inst, 4, k, dots_b.at[step, zi], dots_b.at[step, zi], along_z(k)
+        )))
+
+        @pl.when(step < 2)
         def _():
-            state[2] = dots_sum(own)
-
+            arrive(scatter_copies(inst))
+            depth_sum(inst)
+            gather_private(gathered_w)
+            arrive(depth_copies(inst))
+            full[inst, rows_of(i)] = depth_total(inst)
+            start(share_copies(inst))
+
+        arrive(dots_second)
+        total = dots_b[step, 0]
+        for k in range(1, GROUP):
+            total = total + dots_b[step, k]
+        dots = jnp.transpose(jnp.concatenate([total, jnp.zeros((ED - 8, ED), F32)], axis=0))[:PLANES]
         r_int = r8[TILES - 1]
-        rr = state[2, :, 0:1] + jnp.sum(r_int * r_int, axis=1, keepdims=True)
-        rw = state[2, :, 1:2]
-        ra = state[2, :, 2:3] + jnp.sum(r_int * a8[TILES - 1], axis=1, keepdims=True)
+        rr = dots[:, 0:1] + jnp.sum(r_int * r_int, axis=1, keepdims=True)
+        rw = dots[:, 1:2]
+        ra = dots[:, 2:3] + jnp.sum(r_int * a8[TILES - 1], axis=1, keepdims=True)
         beta = jnp.where(step == 0, 0.0, rr / state[0, :, 0:1])
         energy = rw + 2.0 * beta * ra + beta * beta * state[1, :, 0:1]
         state[0] = jnp.broadcast_to(rr, (PLANES, ED))
@@ -445,11 +464,22 @@
         factors[0] = jnp.broadcast_to(rr / energy, (PLANES, TILE))
         factors[1] = jnp.broadcast_to(beta, (PLANES, TILE))
 
+        def advance(t, values):
+            image = values + factors[1] * a8[t]
+            a8[t] = image
+            r8[t] = r8[t] - factors[0] * image
+
+        @pl.loop(0, TILES)
+        def _(t):
+            direction = r8[t] + factors[1] * p8[t]
+            p8[t] = direction
+            x8[t] = x8[t] + factors[0] * direction
+
         @pl.when(step < 2)
         def _():
-            w_int = full[step + 1, :, :TILE]
-            w8[TILES - 1] = w_int
-            gather_interface(gathered_w, w_int)
+            @pl.loop(0, TILES - 1)
+            def _(t):
+                advance(t, w8[t])
 
             @pl.loop(0, NBE, unroll=2)
             def _(b):
@@ -457,14 +487,17 @@
                 gathered_a[b] = image
                 gathered_r[b] = gathered_r[b] - factors[0, :, :ED] * image
 
-        @pl.loop(0, TILES)
-        def _(t):
-            direction = r8[t] + factors[1] * p8[t]
-            p8[t] = direction
-            x8[t] = x8[t] + factors[0] * direction
-            image = w8[t] + factors[1] * a8[t]
-            a8[t] = image
-            r8[t] = r8[t] - factors[0] * image
+            arrive(share_copies(inst))
+            advance(TILES - 1, full[inst])
+
+            def add(b, values):
+                gathered_a[b] += values
+                gathered_r[b] = gathered_r[b] - factors[0, :, :ED] * values
+
+            gather_interface(add, full[inst])
+            leave(scatter_copies(inst), depth_copies(inst), share_copies(inst))
+
+        leave(dots_first, dots_second)
 
     @pl.loop(0, TILES)
     def _(t):
@@ -516,19 +549,19 @@
             pltpu.VMEM((2, SIZE, TILE), F32),
             pltpu.VMEM((2, SIZE, TILE), F32),
             pltpu.VMEM((GROUP, SPAN, 8, TILE), F32),
-            pltpu.VMEM((3, PLANES, WIDE), F32),
-            pltpu.VMEM((3, GROUP, 8, WIDE), F32),
-            pltpu.VMEM((3, GROUP, 8, WIDE), F32),
-            pltpu.VMEM((3, PLANES, WIDE), F32),
-            pltpu.VMEM((GROUP, 8, ED), F32),
-            pltpu.VMEM((GROUP, 8, ED), F32),
+            pltpu.VMEM((3, PLANES, TILE), F32),
+            pltpu.VMEM((3, GROUP, 8, TILE), F32),
+            pltpu.VMEM((3, GROUP, 8, TILE), F32),
+            pltpu.VMEM((3, PLANES, TILE), F32),
+            pltpu.VMEM((3, GROUP, 8, ED), F32),
+            pltpu.VMEM((3, GROUP, 8, ED), F32),
             pltpu.VMEM((2, PLANES, TILE), F32),
-            pltpu.VMEM((3, PLANES, ED), F32),
+            pltpu.VMEM((2, PLANES, ED), F32),
             pltpu.SemaphoreType.DMA((22,)),
             pltpu.SemaphoreType.DMA((3, SPAN)),
             pltpu.SemaphoreType.DMA((3, SPAN)),
-            pltpu.SemaphoreType.DMA((3, 4, GROUP)),
-            pltpu.SemaphoreType.DMA((3, 4, GROUP)),
+            pltpu.SemaphoreType.DMA((4, 5, GROUP)),
+            pltpu.SemaphoreType.DMA((4, 5, GROUP)),
         ],
         compiler_params=pltpu.CompilerParams(
             collective_id=0, has_side_effects=True, vmem_limit_bytes=62 * 1024 * 1024

time: 102 us -> 101 us (level)
  Pallas kernels: 101 us -> 99.8 us
    pallas_call x1, Pallas kernels: 99 us -> 97.9 us  [shards(): pl.pallas_call(kernel, out_shape=jax.ShapeDtypeStruct((TILES * TILE // ED...]
where the time goes in v3:
time: 101 us; the launch traced here: 100 us
  Pallas kernels  99.8 us (99%)
    pallas_call x1, Pallas kernels, shards(): pl.pallas_call(kernel, out_shape=jax.ShapeDtypeStruct((TILES * TILE // ED...  97.9 us

profile of v3, /device:TPU:1, one launch (start us, length us, event | category | flops | bytes accessed | tf_op | source)
XLA Modules:
  0.0 100.4 jit_solution(508791783486895160)
XLA Ops:
  0.6 97.9 %shard_map.104.slabs = f32[16,64,128]{2,1,0:T(8,128)} custom-call(bf16[3,5184,128]{2,1,0:T(8,128)(2,1)} %bitcast.8, bf16[3,5184,128]{2,1,0:T(8,128)(2,1)} %bitcast.9, f32[32,81]{1,0:T(8,128)} %bitcast.10, f32[1,128]{1,0:T(1,128)} %bitcast.11, s32[32,128]{1,0:T(8,128)} %bmap.1, f32[32,32,128]{2,1,0:T(8,128)} %stiff_hbm.1, f32[32,32,128]{2,1,0:T(8,128)} %mass_hbm.1, ...), custom_call_target="tpu_custom_call" | custom-call | tf_op jit(solution)/shard_map/pallas_call | solution.py:532
  98.6 1.9 %shard_map.105 = (f32[64,1792]{1,0:T(8,128)}, f32[64,256]{1,0:T(8,128)}) custom-call(f32[16,64,128]{2,1,0:T(8,128)} %shard_map.104.slabs), custom_call_target="tpu_custom_call" | custom-call | tf_op jit(solution)/shard_map/pallas_call | solution.py:580

commit v4 on v3

--- a/solution.py
+++ b/solution.py
@@ -238,7 +238,8 @@
         return across(0, k, w8.at[pl.ds(2 * lax.rem(s + k, SPAN), 2)], cross.at[:, rows])
 
     @pl.loop(1, SPAN + 1)
-    def _(k):
+    def _(turn):
+        k = turn + jnp.where(turn == 1, 1, jnp.where(turn == 2, -1, 0))
         j = lax.rem(s + k, SPAN)
         chunk = both(dot(parts[...], rows_hot[:, pl.ds(pl.multiple_of(j * 2 * TILE, 2 * TILE), 2 * TILE)]))
         for half in range(2):
@@ -410,15 +411,20 @@
             total = total + left[t] * right[t]
         return jnp.sum(total, axis=1, keepdims=True)
 
+    def keep_dots():
+        rr = product_sum(r8, r8)
+        ra = product_sum(r8, a8)
+        state[2] = jnp.where(lane == 0, rr, jnp.where(lane == 2, ra, 0.0))
+
     state[0] = jnp.ones((PLANES, ED), F32)
     state[1] = jnp.zeros((PLANES, ED), F32)
+
+    keep_dots()
 
     @pl.loop(0, 3)
     def _(step):
         rw = operate(gathered_r)
-        rr = product_sum(r8, r8)
-        ra = product_sum(r8, a8)
-        own = jnp.where(lane == 0, rr, jnp.where(lane == 1, rw, jnp.where(lane == 2, ra, 0.0)))
+        own = jnp.where(lane == 1, rw, state[2])
 
         inst = step + 1
         dots_a[step, i] = jnp.transpose(jnp.concatenate([own, jnp.zeros_like(own)], axis=0))[:8]
@@ -487,6 +493,7 @@
                 gathered_a[b] = image
                 gathered_r[b] = gathered_r[b] - factors[0, :, :ED] * image
 
+            keep_dots()
             arrive(share_copies(inst))
             advance(TILES - 1, full[inst])
 
@@ -556,7 +563,7 @@
             pltpu.VMEM((3, GROUP, 8, ED), F32),
             pltpu.VMEM((3, GROUP, 8, ED), F32),
             pltpu.VMEM((2, PLANES, TILE), F32),
-            pltpu.VMEM((2, PLANES, ED), F32),
+            pltpu.VMEM((3, PLANES, ED), F32),
             pltpu.SemaphoreType.DMA((22,)),
             pltpu.SemaphoreType.DMA((3, SPAN)),
             pltpu.SemaphoreType.DMA((3, SPAN)),

time: 101 us -> 100 us (0.990)
  no operation moved by 1% of the time
where the time goes in v4:
time: 100 us
  Pallas kernels  99.5 us (100%)
    pallas_call x1, Pallas kernels, shards(): pl.pallas_call(kernel, out_shape=jax.ShapeDtypeStruct((TILES * TILE // ED...  97.6 us

profile of v4, /device:TPU:1, one launch (start us, length us, event | category | flops | bytes accessed | tf_op | source)
XLA Modules:
  0.0 100.1 jit_solution(10479164862145415700)
XLA Ops:
  0.6 97.6 %shard_map.104.slabs = f32[16,64,128]{2,1,0:T(8,128)} custom-call(bf16[3,5184,128]{2,1,0:T(8,128)(2,1)} %bitcast.8, bf16[3,5184,128]{2,1,0:T(8,128)(2,1)} %bitcast.9, f32[32,81]{1,0:T(8,128)} %bitcast.10, f32[1,128]{1,0:T(1,128)} %bitcast.11, s32[32,128]{1,0:T(8,128)} %bmap.1, f32[32,32,128]{2,1,0:T(8,128)} %stiff_hbm.1, f32[32,32,128]{2,1,0:T(8,128)} %mass_hbm.1, ...), custom_call_target="tpu_custom_call" | custom-call | tf_op jit(solution)/shard_map/pallas_call | solution.py:539
  98.2 1.9 %shard_map.105 = (f32[64,1792]{1,0:T(8,128)}, f32[64,256]{1,0:T(8,128)}) custom-call(f32[16,64,128]{2,1,0:T(8,128)} %shard_map.104.slabs), custom_call_target="tpu_custom_call" | custom-call | tf_op jit(solution)/shard_map/pallas_call | solution.py:587
